TPU v7x, 512 devices: a whole 4x4x16 slice. The times are simulated.
512 devices in a mesh: depth: 64 (over z_lo, y, core), chan: 8 (over x, z_hi).
Axes of the slice: x: 4, y: 4, z: 16 (z_hi: 2, z_lo: 8; z = z_hi * 8 + z_lo), core: 2. Of those that a mesh axis runs over, the one named last changes fastest.
Arguments:
- sample: bfloat16 [128, 128, 16, 128], P('chan', 'depth'), may hold values from -6 to 6
- first_weight: bfloat16 [256, 3456], P('chan'), may hold values from -0.109375 to 0.109375
- second_weight: bfloat16 [256, 6912], P('chan'), may hold values from -0.078125 to 0.078125
- cotangent: bfloat16 [256, 64, 8, 64], P('chan', 'depth'), may hold values from -0.023925781 to 0.023925781
Outputs:
- second_out: bfloat16 [256, 64, 8, 64], P('chan', 'depth')
- first_grad: float32 [256, 3456], P('chan', 'depth')
- second_grad: float32 [256, 6912], P('chan', 'depth')
All inputs are finite; a program needn't handle non-finite values.
Results may differ from a plain program's by a relative error of at most 0.017.
Values may be sent and summed in bfloat16 or wider, within the bound.
A program may use at most 64 MiB of HBM per device.

v0:
```python
import jax
import jax.numpy as jnp
from jax import lax
from jax.sharding import PartitionSpec as P

LEAK = 0.3


def passed_along(value, axis, by):
    length = lax.axis_size(axis)
    pairs = [(i, i + by) for i in range(length) if 0 <= i + by < length]
    return lax.ppermute(value, axis, pairs)


def padded_2(cells, sides, width):
    for axis, dim in sides:
        count = lax.axis_size(axis)
        ends = count - 1
        head = lax.slice_in_dim(cells, 0, width, axis=dim)
        tail = lax.slice_in_dim(cells, cells.shape[dim] - width, cells.shape[dim], axis=dim)
        cells = jnp.concatenate(
            [
                lax.ppermute(tail, axis, [(i, (i + 1) % count) for i in range(ends)]),
                cells,
                lax.ppermute(head, axis, [((i + 1) % count, i) for i in range(ends)]),
            ],
            axis=dim,
        )
    return cells


def convolve(inputs, kernel, stride):
    return lax.conv_general_dilated(
        inputs[None],
        kernel,
        (stride, stride, stride),
        ((0, 0), (1, 1), (1, 1)),
        dimension_numbers=("NCDHW", "OIDHW", "NCDHW"),
        preferred_element_type=jnp.float32,
    )[0]


def as_kernel(weight, channels):
    return weight.reshape(weight.shape[0], 3, 3, 3, channels).transpose(0, 4, 1, 2, 3)


def tap_grads(grad_rows, padded, stride, depth_len, height, width):
    pieces = []
    for kd in range(3):
        for kh in range(3):
            for kw in range(3):
                piece = padded[
                    :,
                    kd : kd + stride * depth_len : stride,
                    kh : kh + stride * height : stride,
                    kw : kw + stride * width : stride,
                ]
                flat = piece.reshape(piece.shape[0], -1)
                pieces.append(jnp.dot(grad_rows, flat.T, preferred_element_type=jnp.float32))
    stacked = jnp.stack(pieces, axis=1)
    return stacked.reshape(stacked.shape[0], -1)


def shards(sample, first_weight, second_weight, cotangent):
    rim = passed_along(sample[:, -1:], "depth", 1)
    extended = jnp.concatenate([rim, sample], axis=1)
    gathered = lax.all_gather(extended, "chan", axis=0, tiled=True)
    first_kernel = as_kernel(first_weight, gathered.shape[0])
    first_pre = convolve(gathered, first_kernel, 2)
    slope = jnp.where(first_pre > 0, 1.0, LEAK)
    first_act = (first_pre * slope).astype(jnp.bfloat16)
    act_faces = padded_2(first_act, (("depth", 1),), 1)
    act_all = lax.all_gather(act_faces, "chan", axis=0, tiled=True)
    second_kernel = as_kernel(second_weight, act_all.shape[0])
    second_out = convolve(act_all, second_kernel, 1).astype(jnp.bfloat16)
    grad_faces = padded_2(cotangent, (("depth", 1),), 1)
    flipped = second_kernel.transpose(1, 0, 2, 3, 4)[:, :, ::-1, ::-1, ::-1]
    part = lax.slice_in_dim(flipped, 0, lax.axis_size("chan") * first_act.shape[0], axis=0)
    act_grad = lax.psum_scatter(
        convolve(grad_faces, part, 1).astype(jnp.bfloat16), "chan", scatter_dimension=0, tiled=True
    ).astype(jnp.float32)
    pre_grad = (act_grad * slope).astype(jnp.bfloat16)
    out_planes = first_act.shape[1]
    height = first_act.shape[2]
    width = first_act.shape[3]
    act_pad = jnp.pad(act_all, ((0, 0), (0, 0), (1, 1), (1, 1)))
    second_part = tap_grads(
        cotangent.reshape(cotangent.shape[0], -1), act_pad, 1, out_planes, height, width
    )
    sample_pad = jnp.pad(gathered, ((0, 0), (0, 0), (1, 1), (1, 1)))
    first_part = tap_grads(
        pre_grad.reshape(pre_grad.shape[0], -1), sample_pad, 2, out_planes, height, width
    )
    slabs = lax.axis_size("depth")
    second_total = lax.psum(second_part, "depth")
    first_total = lax.psum(first_part, "depth")
    second_cols = second_part.shape[1] // slabs
    first_cols = first_part.shape[1] // slabs
    second_grad = lax.dynamic_slice_in_dim(
        second_total, lax.axis_index("depth") * second_cols, second_cols, 1
    )
    first_grad = lax.dynamic_slice_in_dim(
        first_total, lax.axis_index("depth") * first_cols, first_cols, 1
    )
    return (second_out, first_grad, second_grad)


def solution(mesh):
    return jax.shard_map(
        shards,
        mesh=mesh,
        in_specs=(
            P("chan", "depth", None, None),
            P("chan", None),
            P("chan", None),
            P("chan", "depth", None, None),
        ),
        out_specs=(P("chan", "depth", None, None), P("chan", "depth"), P("chan", "depth")),
        check_vma=False,
    )
```

profile of v0, /device:TPU:1, one launch (start us, length us, event | category | flops | bytes accessed | tf_op | source)
XLA Modules:
  0.0 1273.6 jit_solution(17362298855732969646)
XLA Ops:
  8.2 8.8 collective-permute-start.4
  17.0 1.9 collective-permute-start.3
  18.9 1.6 reshape.357
  23.9 4.4 collective-permute-start
  28.3 1.3 collective-permute-done
  30.5 106.8 %reduce-scatter.2.cloned.1.call-done = bf16[32,1,8,64]{3,2,1,0:T(8,128)(2,1)} async-done(((bf16[256,1,8,64]{3,2,1,0:T(8,128)(2,1)}), bf16[32,1,8,64]{3,2,1,0:T(8,128)(2,1)}) %reduce-scatter.2.cloned.1.call-update) | async-done | bytes 32784 | tf_op jit(solution)/shard_map/reduce_scatter | solution.py:79
  138.3 99.0 %all-gather.2.cloned.1.call-done = bf16[128,3,16,128]{3,2,1,0:T(8,128)(2,1)} async-done(((bf16[16,3,16,128]{3,2,1,0:T(8,128)(2,1)}), bf16[128,3,16,128]{3,2,1,0:T(8,128)(2,1)}) %all-gather.2.cloned.1.call-update) | async-done | bytes 1572880 | tf_op jit(solution)/shard_map/all_gather | solution.py:67
  237.3 2.7 copy.144
  243.1 4.0 collective-permute-start.2
  247.1 3.0 collective-permute-start.1
  250.1 1.3 copy.164
  252.0 2.5 slice.196
  254.6 2.5 slice.197
  257.1 2.5 slice.198
  259.6 2.5 slice.199
  262.1 2.5 slice.200
  264.6 2.5 slice.201
  267.1 2.5 slice.202
  269.6 2.5 slice.203
  272.1 2.5 slice.204
  274.6 2.5 slice.205
  277.1 2.5 slice.206
  279.6 2.5 slice.207
  282.1 2.5 slice.208
  284.6 2.5 slice.209
  287.1 2.5 slice.210
  289.6 2.5 slice.211
  308.2 135.0 %all_gather.7 = bf16[256,3,8,64]{3,2,1,0:T(8,128)(2,1)S(1)} all-gather(bf16[32,3,8,64]{3,2,1,0:T(8,128)(2,1)S(1)} %copy.149), channel_id=1, replica_groups=mesh['depth'=64,'chan'=8] {'chan'}, dimensions={0}, use_global_device_ids=true | all-gather | bytes 884736 | tf_op jit(solution)/shard_map/all_gather | solution.py:73
  453.0 2.2 fusion.7
  456.0 808.2 %all-reduce.5.cloned.1.call-done = (f32[32,3456]{1,0:T(8,128)}, f32[32,6912]{1,0:T(8,128)}) async-done(((f32[32,3456]{1,0:T(8,128)}, f32[32,6912]{1,0:T(8,128)}), (f32[32,3456]{1,0:T(8,128)}, f32[32,6912]{1,0:T(8,128)})) %all-reduce.5.cloned.1.call-update) | async-done | bytes 1327120 | tf_op jit(solution)/shard_map/psum | solution.py:96
  1264.2 1.4 constant_dynamic-slice_fusion.1
  1265.7 1.4 constant_dynamic-slice_fusion
  (146 shorter events, 36.0 us)
Async XLA Ops:
  7.2 130.1 %reduce-scatter.2.cloned.1.call-start = ((), (), s32[]{:S(2)}) async-start(), calls=%async_computation.2 | async-start | bytes 589824 | tf_op jit(solution)/shard_map/reduce_scatter | solution.py:79
  8.2 12.3 collective-permute-start.4
  17.0 3.9 collective-permute-start.3
  20.5 0.8 copy-start.2
  21.0 0.7 copy-start.18
  22.5 1.4 copy-start.16
  22.6 7.8 copy-start.17
  23.9 213.5 %all-gather.2.cloned.1.call-start = ((), (), s32[]{:S(2)}) async-start(), calls=%async_computation.1 | async-start | bytes 1769472 | tf_op jit(solution)/shard_map/all_gather | solution.py:67
  23.9 5.7 collective-permute-start
  30.4 1233.9 %all-reduce.5.cloned.1.call-start = ((), (), s32[]{:S(2)}) async-start(), calls=%async_computation.3 | async-start | bytes 2654208 | tf_op jit(solution)/shard_map/psum | solution.py:96
  241.1 9.1 copy-start.1
  243.1 63.7 %collective-permute-start.2 = (bf16[32,1,8,64]{0,2,3,1:T(8,128)(2,1)}, bf16[32,1,8,64]{0,2,3,1:T(8,128)(2,1)}, u32[]{:S(2)}, u32[]{:S(2)}) collective-permute-start(bf16[32,1,8,64]{0,2,3,1:T(8,128)(2,1)} %get-tuple-element.12), channel_id=1, source_target_pairs={{8,0},{16,8},{24,16},{32,24},{40,32},{48,40},{56,48},{64,56},{72,6... | collective-permute-start | bytes 98312 | tf_op jit(solution)/shard_map/ppermute | solution.py:25
  247.1 59.7 %collective-permute-start.1 = (bf16[32,1,8,64]{0,2,3,1:T(8,128)(2,1)}, bf16[32,1,8,64]{0,2,3,1:T(8,128)(2,1)}, u32[]{:S(2)}, u32[]{:S(2)}) collective-permute-start(bf16[32,1,8,64]{0,2,3,1:T(8,128)(2,1)} %get-tuple-element.12), channel_id=1, source_target_pairs={{0,8},{8,16},{16,24},{24,32},{32,40},{40,48},{48,56},{56,64},{64,7... | collective-permute-start | bytes 98312 | tf_op jit(solution)/shard_map/ppermute | solution.py:23
  293.0 2.6 copy-start.4
  295.5 6.0 copy-start.15
  295.5 6.2 copy-start.14
  295.5 6.4 copy-start.13
  295.6 6.6 copy-start.12
  295.6 6.8 copy-start.11
  295.7 6.8 copy-start.10
  296.9 5.8 copy-start.9
  298.1 4.9 copy-start.8
  299.2 3.9 copy-start.7
  300.4 3.0 copy-start.6
  301.5 2.0 copy-start.5
  443.3 1.0 copy-start
  451.9 1.1 copy-start.3
Sparse Core Ops, SparseCore 0:
  24.0 113.2 reduce-scatter.1
  141.0 96.3 all-gather.1
  450.8 813.3 all-reduce.4
where the time goes:
time: 1270 us
  waiting for transfers between devices  1020 us (80%)
  blocking collectives  135 us (11%)
  local copies, waits for them, and re-layouts  63.9 us (5%)
  starting transfers between devices  22.2 us (2%)
  matrix products  19.5 us (2%)
  between operations  14.6 us (1%)
    psum x1, waiting for transfers between devices, shards(): first_total = lax.psum(first_part, 'depth')  808 us
    all_gather x1, blocking collectives, shards(): act_all = lax.all_gather(act_faces, 'chan', axis=0, tiled=True)  135 us
    reduce_scatter x1, waiting for transfers between devices, shards(): lax.psum_scatter(convolve(grad_faces, part, 1).astype(jnp.bfloat16), 'cha...  107 us
    all_gather x1, waiting for transfers between devices, shards(): gathered = lax.all_gather(extended, 'chan', axis=0, tiled=True)  99 us
    slice x27, local copies, waits for them, and re-layouts, tap_grads(): padded[:, kd:kd + stride * depth_len:stride, kh:kh + stride * height:stri...  43.4 us
  transfers between devices with their start and end apart: 8, of which 5 were waited for; matrix products, arithmetic and copies ran while one was open for 5% of the time, Pallas kernels for 0%

commit v1 on v0

v1 whole, which is shorter than its diff:
```python
import jax
import jax.numpy as jnp
from jax import lax
from jax.experimental import pallas as pl
from jax.experimental.pallas import tpu as pltpu
from jax.sharding import PartitionSpec as P

LEAK = 0.3
F32 = jnp.float32
BF16 = jnp.bfloat16
MESH = pl.DeviceIdType.MESH

NZ, NY, NK, NX = 8, 4, 2, 4
DEPTH = NZ * NY * NK

S_SAMPLE = 0
S_ACT = 14
S_COT = 28
S_AGX = 30
S_AGZ = 33
S_B1 = 34
S_PG = 35
S_Y = 36
S_CORE = 38
S_YS = 39
S_ZS = 42
N_SEM = 49


def dot(a, b):
    return lax.dot_general(a, b, (((1,), (0,)), ((), ())), preferred_element_type=F32)


def dot_t(a, b):
    return lax.dot_general(a, b, (((1,), (1,)), ((), ())), preferred_element_type=F32)


def shift_matrix(rows, base):
    r = lax.broadcasted_iota(jnp.int32, (rows, 384), 0)
    c = lax.broadcasted_iota(jnp.int32, (rows, 384), 1)
    kw = c >> 7
    m = c & 127
    w = (m & 63) + kw - 1
    hit = (r == m + base + kw - 1) & (w >= 0) & (w < 64)
    return jnp.where(hit, 1.0, 0.0).astype(BF16)


def stride_matrix():
    r = lax.broadcasted_iota(jnp.int32, (256, 384), 0)
    c = lax.broadcasted_iota(jnp.int32, (256, 384), 1)
    kw = c >> 7
    i = (c >> 6) & 1
    w = 2 * (c & 63) + kw - 1
    hit = (r == i * 128 + w) & (w >= 0)
    return jnp.where(hit, 1.0, 0.0).astype(BF16)


def kernel(
    samp, w1, w2, cot,
    so, fgo, sgo,
    g, s, c3, ci, wv, ag32, agb, agr, az32, azb, azr, w1s, b1s, b1r, slope, act, pg2, x9, w2s, ys, yr,
    rsg, rfg, t, cr, u, yrs, v, zr, send_sems, recv_sems,
):
    d = lax.axis_index("depth")
    c = lax.axis_index("chan")
    core = lax.rem(d, 2)
    y = lax.rem(d // 2, NY)
    zl = d // (2 * NY)
    x = c // 2
    zh = lax.rem(c, 2)
    first = d == 0
    last = d == DEPTH - 1

    def chan_at(dx, flip=False):
        return lax.rem(x + dx + NX, NX) * 2 + (1 - zh if flip else zh)

    xdev = [(d, chan_at(k)) for k in (1, 2, 3)]
    zdev = (d, chan_at(0, True))
    kdev = (d + 1 - 2 * core, c)
    ydev = [(zl * 8 + lax.rem(y + k, NY) * 2 + core, c) for k in (1, 2, 3)]
    zldev = [(lax.rem(zl + k, NZ) * 8 + y * 2 + core, c) for k in range(1, 8)]
    up = (lax.rem(d + 1, DEPTH), c)
    down = (lax.rem(d + DEPTH - 1, DEPTH), c)
    right, left = xdev[0], xdev[2]

    pending = []

    def desc(k, src, dst, dev):
        return pltpu.make_async_remote_copy(
            src_ref=src, dst_ref=dst, send_sem=send_sems.at[k], recv_sem=recv_sems.at[k], device_id=dev, device_id_type=MESH
        )

    def send(k, src, dst, dev, cond=None):
        copy = desc(k, src, dst, dev)
        if cond is None:
            copy.start()
        else:
            pl.when(cond)(copy.start)
        pending.append((copy, cond))

    def recv(k, dst, dev, cond=None):
        copy = desc(k, dst, dst, dev)
        if cond is None:
            copy.wait_recv()
        else:
            pl.when(cond)(copy.wait_recv)

    c3[...] = jnp.zeros(c3.shape, BF16)
    act[:, 0:128] = jnp.zeros((256, 128), BF16)
    act[:, 640:768] = jnp.zeros((256, 128), BF16)
    g[32] = jnp.zeros((128, 128), BF16)

    @pl.when(first)
    def _():
        b1r[...] = jnp.zeros(b1r.shape, F32)
        yr[0] = jnp.zeros((32, 512), BF16)

    @pl.when(last)
    def _():
        pg2[32:64] = jnp.zeros((32, 512), BF16)
        yr[1] = jnp.zeros((32, 512), BF16)

    barrier = pltpu.get_barrier_semaphore()
    partners = xdev + [zdev, kdev] + ydev + zldev + [up, down]
    for dev in partners:
        pl.semaphore_signal(barrier, inc=1, device_id=dev, device_id_type=MESH)
    pl.semaphore_wait(barrier, len(partners))

    class Gather:
        def __init__(self, base, own, block):
            self.base, self.own, self.block = base, own, block

        def start(self):
            for i in range(2):
                send(self.base + i, self.own(i), self.block(c, i), zdev)
            for i in range(2):
                send(self.base + 2 + i, self.own(i), self.block(c, i), right)
                send(self.base + 4 + 1 - i, self.own(1 - i), self.block(c, 1 - i), left)

        def relay_x(self):
            b, blk = self.base, self.block
            from_left = blk(chan_at(-1), 0)
            recv(b + 2, from_left, left)
            send(b + 6, from_left, from_left, right)
            from_right = blk(chan_at(1), 1)
            recv(b + 5, from_right, right)
            send(b + 7, from_right, from_right, left)

        def relay_z(self, i):
            b, blk = self.base, self.block
            over = blk(chan_at(0, True), i)
            recv(b + i, over, zdev)
            send(b + 8 + i, over, over, right)
            send(b + 10 + i, over, over, left)

        def relay_zx(self):
            b, blk = self.base, self.block
            from_left = blk(chan_at(-1, True), 0)
            recv(b + 8, from_left, left)
            send(b + 12, from_left, from_left, right)
            from_right = blk(chan_at(1, True), 1)
            recv(b + 11, from_right, right)
            send(b + 13, from_right, from_right, left)

        def finish(self):
            b, blk = self.base, self.block
            recv(b + 3, blk(chan_at(-1), 1), left)
            recv(b + 4, blk(chan_at(1), 0), right)
            recv(b + 6, blk(chan_at(2), 0), left)
            recv(b + 7, blk(chan_at(2), 1), right)
            recv(b + 9, blk(chan_at(-1, True), 1), left)
            recv(b + 10, blk(chan_at(1, True), 0), right)
            recv(b + 12, blk(chan_at(2, True), 0), left)
            recv(b + 13, blk(chan_at(2, True), 1), right)

    sample_gather = Gather(
        S_SAMPLE,
        lambda i: samp.at[16 * i : 16 * i + 16],
        lambda r, i: g.at[16 * i : 16 * i + 16, pl.ds(pl.multiple_of(r * 16, 16), 16), :],
    )
    act_gather = Gather(
        S_ACT,
        lambda i: act.at[pl.ds(pl.multiple_of(c * 32 + 16 * i, 16), 16), 128:640],
        lambda r, i: act.at[pl.ds(pl.multiple_of(r * 32 + 16 * i, 16), 16), 128:640],
    )

    send(S_COT, cot, c3.at[64:96, 128:640], up, jnp.logical_not(last))
    send(S_COT + 1, cot, c3.at[0:32, 128:640], down, jnp.logical_not(first))
    sample_gather.start()

    c3[32:64, 128:640] = cot[...]
    g[0:32, pl.ds(pl.multiple_of(c * 16, 16), 16), :] = samp[...]
    for k in range(27):
        wv[32 * k : 32 * k + 32] = w2[:, 256 * k : 256 * k + 256]
    for k in range(3):
        w2s[32 * k : 32 * k + 32] = w2[:, 2304 * k : 2304 * k + 2304]
    w1s[0:32] = w1[:, 2304:3456]
    w1s[32:64] = w1[:, 0:1152]
    sh_two = shift_matrix(256, 64)
    sh_one = shift_matrix(128, 0)
    recv(S_COT, c3.at[64:96, 128:640], down, jnp.logical_not(first))
    recv(S_COT + 1, c3.at[0:32, 128:640], up, jnp.logical_not(last))

    def shifted(ref, j, kh):
        if kh == 1:
            return dot(ref[:, 128 * (j + 1) : 128 * (j + 2)], sh_one).astype(BF16)
        at = 128 * j if kh == 0 else 128 * (j + 1)
        return dot(ref[:, at : at + 256], sh_two).astype(BF16)

    for j in range(4):
        for kh in range(3):
            tile = shifted(c3, j, kh)
            for kw in range(3):
                for kd in range(3):
                    tap = 9 * kd + 3 * (2 - kh) + 2 - kw
                    ci[32 * tap : 32 * tap + 32, 128 * j : 128 * j + 128] = tile[32 * kd : 32 * kd + 32, 128 * kw : 128 * kw + 128]
    part = lax.dot_general(wv[...], ci[...], (((0,), (0,)), ((), ())), preferred_element_type=F32)
    ag32[...] = part
    agb[...] = part.astype(BF16)

    sample_gather.relay_x()
    for k in range(3):
        to = lax.rem(x + k + 1, NX)
        send(S_AGX + k, agb.at[pl.ds(pl.multiple_of(to * 64, 64), 64)], agr.at[k], xdev[k])
    sample_gather.relay_z(0)
    total = ag32[pl.ds(pl.multiple_of(x * 64, 64), 64)]
    for k in range(3):
        recv(S_AGX + k, agr.at[k], xdev[2 - k])
        total = total + agr[k].astype(F32)
    az32[...] = total
    azb[...] = total.astype(BF16)
    send(S_AGZ, azb.at[pl.ds(pl.multiple_of((1 - zh) * 32, 32), 32)], azr, zdev)
    sample_gather.relay_z(1)
    sample_gather.relay_zx()
    sample_gather.finish()

    stride = stride_matrix()
    for plane in (1, 0):
        for j in range(4):
            for kh in range(3):
                at = 4 * j + kh - 1
                low = g[16 * plane + at] if at >= 0 else g[32]
                tile = dot(jnp.concatenate([low, g[16 * plane + at + 2]], axis=1), stride).astype(BF16)
                for kw in range(3):
                    row = 128 * (3 * kh + kw)
                    s[plane, row : row + 128, 128 * j : 128 * j + 128] = tile[:, 128 * kw : 128 * kw + 128]
        if plane == 1:
            both = dot(w1s[...], s[1])
            b1s[...] = both[32:64]
            send(S_B1, b1s, b1r, up, jnp.logical_not(last))
    pre = both[0:32] + dot(w1[:, 1152:2304], s[0])
    recv(S_B1, b1r, down, jnp.logical_not(first))
    pre = pre + b1r[...]
    sl = jnp.where(pre > 0, 1.0, LEAK)
    act[pl.ds(pl.multiple_of(c * 32, 32), 32), 128:640] = (pre * sl).astype(BF16)
    act_gather.start()

    recv(S_AGZ, azr, zdev)
    grad = az32[pl.ds(pl.multiple_of(zh * 32, 32), 32)] + azr[...].astype(F32)
    pg2[0:32] = (grad * sl).astype(BF16)
    send(S_PG, pg2.at[0:32], pg2.at[32:64], down, jnp.logical_not(first))
    act_gather.relay_x()
    rfg[:, 1152:2304] = dot_t(pg2[0:32], s[0])
    rfg[:, 3456:3584] = jnp.zeros((32, 128), F32)
    recv(S_PG, pg2.at[32:64], up, jnp.logical_not(last))
    act_gather.relay_z(0)
    act_gather.relay_z(1)
    both = dot_t(pg2[...], s[1])
    rfg[:, 2304:3456] = both[0:32]
    rfg[:, 0:1152] = both[32:64]
    act_gather.relay_zx()
    act_gather.finish()

    for j in range(4):
        for kh in range(3):
            tile = shifted(act, j, kh)
            for kw in range(3):
                row = 256 * (3 * kh + kw)
                x9[row : row + 256, 128 * j : 128 * j + 128] = tile[:, 128 * kw : 128 * kw + 128]
    out = dot(w2s[...], x9[...])
    ys[0:32] = out[0:32].astype(BF16)
    ys[32:64] = out[64:96].astype(BF16)
    send(S_Y, ys.at[0:32], yr.at[0], up, jnp.logical_not(last))
    send(S_Y + 1, ys.at[32:64], yr.at[1], down, jnp.logical_not(first))
    grads = dot_t(c3[:, 128:640], x9[...])
    rsg[0:32, 0:2304] = grads[0:32]
    rsg[0:32, 2304:3456] = grads[32:64, 0:1152]
    rsg[32:64, 0:1152] = grads[32:64, 1152:2304]
    rsg[32:64, 1152:3456] = grads[64:96]
    rsg[:, 3456:3584] = jnp.zeros((64, 128), F32)

    for k in range(32):
        zz, yy, kk = k // 8, (k % 8) // 2, k % 2
        piece = rsg[:, 108 * k : 108 * k + 128].astype(BF16)
        t[kk, yy, zz] = piece[0:32]
        t[kk, yy, zz + 4] = piece[32:64]
        low = rfg[:, 54 * k : 54 * k + 64]
        high = rfg[:, 54 * (k + 32) : 54 * (k + 32) + 64]
        t[kk, yy, 8 + zz] = jnp.concatenate([low, high], axis=1).astype(BF16)
    send(S_CORE, t.at[1 - core], cr, kdev)
    recv(S_Y, yr.at[0], down, jnp.logical_not(first))
    recv(S_Y + 1, yr.at[1], up, jnp.logical_not(last))
    so[...] = (out[32:64] + yr[0].astype(F32) + yr[1].astype(F32)).astype(BF16)
    recv(S_CORE, cr, kdev)
    u[...] = (t[core].astype(F32) + cr[...].astype(F32)).astype(BF16)
    for k in range(3):
        send(S_YS + k, u.at[lax.rem(y + k + 1, NY)], yrs.at[k], ydev[k])
    total = u[y].astype(F32)
    for k in range(3):
        recv(S_YS + k, yrs.at[k], ydev[2 - k])
        total = total + yrs[k].astype(F32)
    total = total.astype(BF16)
    for k in range(8):
        v[k, 0] = total[k]
        v[k, 1] = total[8 + k % 4]
    for k in range(7):
        send(S_ZS + k, v.at[lax.rem(zl + k + 1, NZ)], zr.at[k], zldev[k])
    total = v[zl].astype(F32)
    for k in range(7):
        recv(S_ZS + k, zr.at[k], zldev[6 - k])
        total = total + zr[k].astype(F32)
    sgo[...] = total[0, :, 0:108]
    fgo[...] = jnp.where(zl < 4, total[1, :, 0:54], total[1, :, 64:118])

    for copy, cond in pending:
        if cond is None:
            copy.wait_send()
        else:
            pl.when(cond)(copy.wait_send)


def shards(sample, first_weight, second_weight, cotangent):
    samp = sample.transpose(1, 2, 0, 3).reshape(32, 16, 128)
    vmem = pl.BlockSpec(memory_space=pltpu.VMEM)
    so, fgo, sgo = pl.pallas_call(
        kernel,
        out_shape=(
            jax.ShapeDtypeStruct((32, 512), BF16),
            jax.ShapeDtypeStruct((32, 54), F32),
            jax.ShapeDtypeStruct((32, 108), F32),
        ),
        in_specs=[vmem] * 4,
        out_specs=(vmem, vmem, vmem),
        scratch_shapes=[
            pltpu.VMEM((33, 128, 128), BF16),
            pltpu.VMEM((2, 1152, 512), BF16),
            pltpu.VMEM((96, 768), BF16),
            pltpu.VMEM((864, 512), BF16),
            pltpu.VMEM((864, 256), BF16),
            pltpu.VMEM((256, 512), F32),
            pltpu.VMEM((256, 512), BF16),
            pltpu.VMEM((3, 64, 512), BF16),
            pltpu.VMEM((64, 512), F32),
            pltpu.VMEM((64, 512), BF16),
            pltpu.VMEM((32, 512), BF16),
            pltpu.VMEM((64, 1152), BF16),
            pltpu.VMEM((32, 512), F32),
            pltpu.VMEM((32, 512), F32),
            pltpu.VMEM((32, 512), F32),
            pltpu.VMEM((256, 768), BF16),
            pltpu.VMEM((64, 512), BF16),
            pltpu.VMEM((2304, 512), BF16),
            pltpu.VMEM((96, 2304), BF16),
            pltpu.VMEM((64, 512), BF16),
            pltpu.VMEM((2, 32, 512), BF16),
            pltpu.VMEM((64, 3584), F32),
            pltpu.VMEM((32, 3584), F32),
            pltpu.VMEM((2, 4, 12, 32, 128), BF16),
            pltpu.VMEM((4, 12, 32, 128), BF16),
            pltpu.VMEM((4, 12, 32, 128), BF16),
            pltpu.VMEM((3, 12, 32, 128), BF16),
            pltpu.VMEM((8, 2, 32, 128), BF16),
            pltpu.VMEM((7, 2, 32, 128), BF16),
            pltpu.SemaphoreType.DMA((N_SEM,)),
            pltpu.SemaphoreType.DMA((N_SEM,)),
        ],
        compiler_params=pltpu.CompilerParams(collective_id=0, has_side_effects=True, vmem_limit_bytes=40 * 1024 * 1024),
        name="slab_pair",
    )(samp, first_weight, second_weight, cotangent.reshape(32, 512))
    return so.reshape(32, 1, 8, 64), fgo, sgo


def solution(mesh):
    return jax.shard_map(
        shards,
        mesh=mesh,
        in_specs=(
            P("chan", "depth", None, None),
            P("chan", None),
            P("chan", None),
            P("chan", "depth", None, None),
        ),
        out_specs=(P("chan", "depth", None, None), P("chan", "depth"), P("chan", "depth")),
        check_vma=False,
    )
```

time: 1270 us -> 79 us (0.06)
  waiting for transfers between devices: 1020 us -> 0 us
  blocking collectives: 135 us -> 0 us
  Pallas kernels: 0 us -> 73.2 us
  local copies, waits for them, and re-layouts: 63.9 us -> 4.91 us
  starting transfers between devices: 22.2 us -> 0 us
  matrix products: 19.5 us -> 0 us
  between operations: 14.6 us -> 0.67 us
    psum x1 -> x0, waiting for transfers between devices: 808 us -> none  [shards(): first_total = lax.psum(first_part, 'depth')]
    all_gather x1 -> x0, blocking collectives: 135 us -> none  [shards(): act_all = lax.all_gather(act_faces, 'chan', axis=0, tiled=True)]
    reduce_scatter x1 -> x0, waiting for transfers between devices: 107 us -> none  [shards(): lax.psum_scatter(convolve(grad_faces, part, 1).astype(jnp.bfloat16), 'cha...]
    all_gather x1 -> x0, waiting for transfers between devices: 99 us -> none  [shards(): gathered = lax.all_gather(extended, 'chan', axis=0, tiled=True)]
    pallas_call x0 -> x1, Pallas kernels: none -> 73.2 us  [shards(): pl.pallas_call(kernel, out_shape=(jax.ShapeDtypeStruct((32, 512), BF16),...]
    slice x28 -> x0, local copies, waits for them, and re-layouts: 43.4 us -> none  [the longest x27 43.4 us: tap_grads(): padded[:, kd:kd + stride * depth_len:stride, kh:kh + stride * height:stri...]
    ppermute x5 -> x0, starting transfers between devices: 22.1 us -> none  [the longest x2 12.8 us: padded_2(): lax.ppermute(head, axis, [((i + 1) % count, i) for i in range(ends)])]
    dot_general x54 -> x0, matrix products: 15.3 us -> none  [tap_grads(): jnp.dot(grad_rows, flat.T, preferred_element_type=jnp.float32)]
  transfers between devices with their start and end apart: 8 -> 0, of which waited for: 5 -> 0; matrix products, arithmetic and copies ran while one was open for 5% -> 0% of each run, Pallas kernels for 0% -> 0%
where the time goes in v1:
time: 79 us; the launch traced here: 78.8 us
  Pallas kernels  73.2 us (93%)
  local copies, waits for them, and re-layouts  4.91 us (6%)
    pallas_call x1, Pallas kernels, shards(): pl.pallas_call(kernel, out_shape=(jax.ShapeDtypeStruct((32, 512), BF16),...  73.2 us
    unnamed x6, local copies, waits for them, and re-layouts  2.22 us

profile of v1, /device:TPU:1, one launch (start us, length us, event | category | flops | bytes accessed | tf_op | source)
XLA Modules:
  0.0 78.8 jit_solution(15281756635715791259)
XLA Ops:
  0.6 0.0 copy-start.1
  0.6 1.0 %reshape.16.cot = bf16[32,512]{1,0:T(8,128)(2,1)S(1)} reshape(bf16[32,1,8,64]{3,2,1,0:T(8,128)(2,1)} %param.7) | data formatting | bytes 65536 | tf_op jit(solution)/shard_map/reshape | solution.py:379
  1.6 1.0 %copy.7 = bf16[2,16,16,128]{3,2,1,0:T(8,128)(2,1)S(1)} copy(bf16[2,16,16,128]{3,1,0,2:T(8,128)(2,1)} %bitcast.6) | data formatting | bytes 262144 | tf_op jit(solution)/shard_map/transpose | solution.py:333
  2.6 0.0 copy-done.1
  2.6 0.0 copy-start
  2.6 1.0 %copy-done = bf16[32,6912]{1,0:T(8,128)(2,1)S(1)} copy-done((bf16[32,6912]{1,0:T(8,128)(2,1)S(1)}, bf16[32,6912]{1,0:T(8,128)(2,1)}, u32[]{:S(2)}) %copy-start) | copy-done | bytes 442392
  3.6 73.2 %slab_pair.1 = (bf16[32,512]{1,0:T(8,128)(2,1)S(1)}, f32[32,54]{1,0:T(8,128)S(1)}, f32[32,108]{1,0:T(8,128)S(1)}) custom-call(bf16[32,16,128]{2,1,0:T(8,128)(2,1)S(1)} %bitcast.5, bf16[32,3456]{1,0:T(8,128)(2,1)S(1)} %copy-done.1, bf16[32,6912]{1,0:T(8,128)(2,1)S(1)} %copy-done, bf16[32,512]{1,0:T(8,128)(2,1)S(1)} %reshape.16.cot), custom_call_target="tpu_custom_call" | custom-call | tf_op jit(solution)/shard_map/slab_pair/pallas_call | solution.py:335
  76.9 0.7 reshape.17
  77.6 0.6 copy.11
  78.2 0.6 copy.12
Async XLA Ops:
  0.6 2.0 %copy-start.1 = (bf16[32,3456]{1,0:T(8,128)(2,1)S(1)}, bf16[32,3456]{1,0:T(8,128)(2,1)}, u32[]{:S(2)}) copy-start(bf16[32,3456]{1,0:T(8,128)(2,1)} %w1.1) | copy-start | bytes 663556
  2.6 1.0 %copy-start = (bf16[32,6912]{1,0:T(8,128)(2,1)S(1)}, bf16[32,6912]{1,0:T(8,128)(2,1)}, u32[]{:S(2)}) copy-start(bf16[32,6912]{1,0:T(8,128)(2,1)} %w2.1) | copy-start | bytes 1327108

commit v2 on v1

v2 whole, which is shorter than its diff:
```python
import jax
import jax.numpy as jnp
from jax import lax
from jax.experimental import pallas as pl
from jax.experimental.pallas import tpu as pltpu
from jax.sharding import PartitionSpec as P

LEAK = 0.3
F32 = jnp.float32
BF16 = jnp.bfloat16
MESH = pl.DeviceIdType.MESH

NZ, NY, NK, NX = 8, 4, 2, 4
DEPTH = NZ * NY * NK

S_Z = 0
S_OX = 3
S_FX = 9
S_ACT = 18
S_COT = 21
S_AGX = 23
S_AGZ = 26
S_B1 = 27
S_PG = 28
S_Y = 29
S_KF = 31
S_KS = 32
S_YF = 33
S_YS = 36
S_ZF = 39
S_ZS = 46
S_WZ = 53
S_WL = 54
S_WY = 61
S_WK = 64
N_SEM = 65

CHUNKS = ((16, 32), (7, 16), (0, 7))


def dot(a, b):
    return lax.dot_general(a, b, (((1,), (0,)), ((), ())), preferred_element_type=F32)


def dot_t(a, b):
    return lax.dot_general(a, b, (((1,), (1,)), ((), ())), preferred_element_type=F32)


def shift_matrix(rows, base):
    r = lax.broadcasted_iota(jnp.int32, (rows, 384), 0)
    c = lax.broadcasted_iota(jnp.int32, (rows, 384), 1)
    kw = c >> 7
    m = c & 127
    w = (m & 63) + kw - 1
    hit = (r == m + base + kw - 1) & (w >= 0) & (w < 64)
    return jnp.where(hit, 1.0, 0.0).astype(BF16)


def stride_matrix():
    r = lax.broadcasted_iota(jnp.int32, (256, 384), 0)
    c = lax.broadcasted_iota(jnp.int32, (256, 384), 1)
    kw = c >> 7
    i = (c >> 6) & 1
    w = 2 * (c & 63) + kw - 1
    hit = (r == i * 128 + w) & (w >= 0)
    return jnp.where(hit, 1.0, 0.0).astype(BF16)


def swap_matrix(rows, fast):
    slow = rows // fast
    bits = slow.bit_length() - 1
    r = lax.broadcasted_iota(jnp.int32, (rows, rows), 0)
    k = lax.broadcasted_iota(jnp.int32, (rows, rows), 1)
    hit = ((k >> bits) == (r & (fast - 1))) & ((k & (slow - 1)) == (r >> (fast.bit_length() - 1)))
    return jnp.where(hit, 1.0, 0.0).astype(BF16)


def kernel(
    samp_hbm, w1_hbm, w2_hbm, cot_hbm,
    so, fgo, sgo,
    sraw, w1, w2, craw, own, cot, g, s, c3, ci, wv, ag32, agb, agr, az32, azb, azr, wo, wp, w1p, w1m, b1s, b1r,
    slope, act, pg2, x9, w2s, ys, yr, rsg, rfg, tf, cf, uf, yf, vf, zf, ts, cs, us, yg, vs, zs,
    send_sems, recv_sems, load_sems,
):
    d = lax.axis_index("depth")
    c = lax.axis_index("chan")
    core = lax.rem(d, 2)
    y = lax.rem(d // 2, NY)
    zl = d // (2 * NY)
    x = c // 2
    zh = lax.rem(c, 2)
    first = d == 0
    last = d == DEPTH - 1

    def chan_at(dx, flip=False):
        return lax.rem(x + dx + NX, NX) * 2 + (1 - zh if flip else zh)

    xdev = [(d, chan_at(k)) for k in (1, 2, 3)]
    zdev = (d, chan_at(0, True))
    kdev = (d + 1 - 2 * core, c)
    ydev = [(zl * 8 + lax.rem(y + k, NY) * 2 + core, c) for k in (1, 2, 3)]
    zldev = [(lax.rem(zl + k, NZ) * 8 + y * 2 + core, c) for k in range(1, 8)]
    up = (lax.rem(d + 1, DEPTH), c)
    down = (lax.rem(d + DEPTH - 1, DEPTH), c)

    barrier = pltpu.get_barrier_semaphore()
    partners = [zdev] + zldev + xdev + ydev + [kdev, up, down]
    for dev in partners:
        pl.semaphore_signal(barrier, inc=1, device_id=dev, device_id_type=MESH)
    loads = [
        pltpu.make_async_copy(src, dst, load_sems.at[i])
        for i, (src, dst) in enumerate(((samp_hbm, sraw), (cot_hbm, craw), (w1_hbm, w1), (w2_hbm, w2)))
    ]
    for load in loads:
        load.start()

    pending = []

    def desc(k, src, dst, dev):
        return pltpu.make_async_remote_copy(
            src_ref=src, dst_ref=dst, send_sem=send_sems.at[k], recv_sem=recv_sems.at[k], device_id=dev, device_id_type=MESH
        )

    def send(k, src, dst, dev, cond=None):
        copy = desc(k, src, dst, dev)
        if cond is None:
            copy.start()
        else:
            pl.when(cond)(copy.start)
        pending.append((copy, cond))

    def recv(k, dst, dev, cond=None):
        copy = desc(k, dst, dst, dev)
        if cond is None:
            copy.wait_recv()
        else:
            pl.when(cond)(copy.wait_recv)

    def rows(start, size):
        return pl.ds(pl.multiple_of(start, size), size)

    def sample_block(r, lines):
        return g.at[lines[0] : lines[1], rows(r * 16, 16), :]

    loads[0].wait()
    swap = swap_matrix(256, 16)
    for plane in range(2):
        lines = dot(swap, sraw[:, plane].reshape(256, 128))
        own[16 * plane : 16 * plane + 16] = lines.astype(BF16).reshape(16, 16, 128)
    loads[1].wait()
    lines = dot(swap_matrix(256, 32), craw[:, 0].astype(F32).reshape(256, 64).astype(BF16))
    for j in range(4):
        pair = jnp.concatenate([lines[64 * j : 64 * j + 32], lines[64 * j + 32 : 64 * j + 64]], axis=1)
        cot[:, 128 * j : 128 * j + 128] = pair.astype(BF16)
    loads[2].wait()
    wo[...] = jnp.zeros(wo.shape, BF16)
    for k in range(27):
        wo[k // 4, k % 4] = w1[:, 128 * k : 128 * k + 128].reshape(2, 16, 128)
    pl.semaphore_wait(barrier, len(partners))

    send(S_WZ, wo.at[zl, y, core], wp.at[zl, y, core], zdev)
    for i, lines in enumerate(CHUNKS):
        send(S_Z + i, own.at[lines[0] : lines[1]], sample_block(c, lines), zdev)
    send(S_COT, cot, c3.at[64:96, 128:640], up, jnp.logical_not(last))
    send(S_COT + 1, cot, c3.at[0:32, 128:640], down, jnp.logical_not(first))
    for i, lines in enumerate(((16, 32), (0, 16))):
        for k in range(3):
            send(S_OX + 3 * i + k, own.at[lines[0] : lines[1]], sample_block(c, lines), xdev[k])

    c3[:, 0:128] = jnp.zeros((96, 128), BF16)
    c3[:, 640:768] = jnp.zeros((96, 128), BF16)
    act[:, 0:128] = jnp.zeros((256, 128), BF16)
    act[:, 640:768] = jnp.zeros((256, 128), BF16)
    g[32] = jnp.zeros((128, 128), BF16)

    @pl.when(first)
    def _():
        c3[64:96, 128:640] = jnp.zeros((32, 512), BF16)

    @pl.when(last)
    def _():
        c3[0:32, 128:640] = jnp.zeros((32, 512), BF16)
        pg2[32:64] = jnp.zeros((32, 512), BF16)

    c3[32:64, 128:640] = cot[...]
    g[0:32, rows(c * 16, 16), :] = own[...]
    loads[3].wait()
    for k in range(27):
        wv[32 * k : 32 * k + 32] = w2[:, 256 * k : 256 * k + 256]
    for k in range(3):
        w2s[32 * k : 32 * k + 32] = w2[:, 2304 * k : 2304 * k + 2304]
    mine = pl.multiple_of(zh * 32, 32)
    theirs = pl.multiple_of((1 - zh) * 32, 32)
    w1p[pl.ds(mine, 32)] = w1[:, 2304:3456]
    w1p[pl.ds(mine + 64, 32)] = w1[:, 0:1152]
    w1m[pl.ds(mine, 32)] = w1[:, 1152:2304]
    sh_two = shift_matrix(256, 64)
    sh_one = shift_matrix(128, 0)
    recv(S_COT, c3.at[64:96, 128:640], down, jnp.logical_not(first))
    recv(S_COT + 1, c3.at[0:32, 128:640], up, jnp.logical_not(last))

    def shifted(ref, j, kh):
        if kh == 1:
            return dot(ref[:, 128 * (j + 1) : 128 * (j + 2)], sh_one).astype(BF16)
        at = 128 * j if kh == 0 else 128 * (j + 1)
        return dot(ref[:, at : at + 256], sh_two).astype(BF16)

    for j in range(4):
        for kh in range(3):
            tile = shifted(c3, j, kh)
            for kw in range(3):
                for kd in range(3):
                    tap = 9 * kd + 3 * (2 - kh) + 2 - kw
                    ci[32 * tap : 32 * tap + 32, 128 * j : 128 * j + 128] = tile[32 * kd : 32 * kd + 32, 128 * kw : 128 * kw + 128]
    part = lax.dot_general(wv[...], ci[...], (((0,), (0,)), ((), ())), preferred_element_type=F32)
    ag32[...] = part
    agb[...] = part.astype(BF16)
    for k in range(3):
        send(S_AGX + k, agb.at[rows(lax.rem(x + k + 1, NX) * 64, 64)], agr.at[k], xdev[k])

    recv(S_WZ, wp.at[zl, y, core], zdev)
    for k in range(7):
        send(S_WL + k, wp.at[zl, y, core], wp.at[zl, y, core], zldev[k])

    total = ag32[rows(x * 64, 64)]
    for k in range(3):
        recv(S_AGX + k, agr.at[k], xdev[2 - k])
        total = total + agr[k].astype(F32)
    az32[...] = total
    azb[...] = total.astype(BF16)
    send(S_AGZ, azb.at[pl.ds(theirs, 32)], azr, zdev)

    def across(i):
        block = sample_block(chan_at(0, True), CHUNKS[i])
        recv(S_Z + i, block, zdev)
        for k in range(3):
            send(S_FX + 3 * i + k, block, block, xdev[k])

    def arrived(i):
        for k in range(3):
            recv(S_FX + 3 * i + k, sample_block(chan_at(3 - k, True), CHUNKS[i]), xdev[2 - k])

    across(0)
    for k in range(7):
        recv(S_WL + k, wp.at[lax.rem(zl + 7 - k, NZ), y, core], zldev[6 - k])
    for k in range(3):
        send(S_WY + k, wp.at[:, y, core], wp.at[:, y, core], ydev[k])
    across(1)
    across(2)
    for i, lines in enumerate(((16, 32), (0, 16))):
        for k in range(3):
            recv(S_OX + 3 * i + k, sample_block(chan_at(3 - k), lines), xdev[2 - k])
    for k in range(3):
        recv(S_WY + k, wp.at[:, lax.rem(y + 3 - k, NY), core], ydev[2 - k])
    send(S_WK, wp.at[:, :, core], wp.at[:, :, core], kdev)
    stride = stride_matrix()

    def strided(plane, j):
        for kh in range(3):
            at = 4 * j + kh - 1
            low = g[16 * plane + at] if at >= 0 else g[32]
            tile = dot(jnp.concatenate([low, g[16 * plane + at + 2]], axis=1), stride).astype(BF16)
            for kw in range(3):
                row = 128 * (3 * kh + kw)
                s[plane, row : row + 128, 128 * j : 128 * j + 128] = tile[:, 128 * kw : 128 * kw + 128]

    arrived(0)
    for j in range(4):
        strided(1, j)
    recv(S_WK, wp.at[:, :, 1 - core], kdev)
    for k in range(27):
        tile = wp[k // 4, k % 4].reshape(32, 128)
        at = 128 * (k % 9)
        if k // 9 == 1:
            w1m[pl.ds(theirs, 32), at : at + 128] = tile
        else:
            w1p[pl.ds(theirs + (64 if k < 9 else 0), 32), at : at + 128] = tile
    both = dot(w1p[...], s[1])
    b1s[...] = both[64:128]
    send(S_B1, b1s, b1r, up, jnp.logical_not(last))
    arrived(1)
    halves = [None, None]
    for half in (1, 0):
        if half == 0:
            arrived(2)
        strided(0, 2 * half)
        strided(0, 2 * half + 1)
        halves[half] = dot(w1m[...], s[0, :, 256 * half : 256 * half + 256])
    pre = both[0:64] + jnp.concatenate(halves, axis=1)
    recv(S_B1, b1r, down, jnp.logical_not(first))
    pre = pre + jnp.where(first, 0.0, b1r[...])
    sl = jnp.where(pre > 0, 1.0, LEAK)
    group = act.at[rows(x * 64, 64), 128:640]
    group[...] = (pre * sl).astype(BF16)
    for k in range(3):
        send(S_ACT + k, group, group, xdev[k])
    slope[...] = sl

    recv(S_AGZ, azr, zdev)
    grad = az32[pl.ds(mine, 32)] + azr[...].astype(F32)
    pg2[0:32] = (grad * slope[pl.ds(mine, 32)]).astype(BF16)
    send(S_PG, pg2.at[0:32], pg2.at[32:64], down, jnp.logical_not(first))
    rfg[:, 1152:2304] = dot_t(pg2[0:32], s[0])
    rfg[:, 3456:3584] = jnp.zeros((32, 128), F32)
    recv(S_PG, pg2.at[32:64], up, jnp.logical_not(last))
    both = dot_t(pg2[...], s[1])
    rfg[:, 2304:3456] = both[0:32]
    rfg[:, 0:1152] = both[32:64]

    for k in range(32):
        low = rfg[:, 54 * k : 54 * k + 64]
        high = rfg[:, 54 * (k + 32) : 54 * (k + 32) + 64]
        tf[k % 2, (k % 8) // 2, k // 8] = jnp.concatenate([low, high], axis=1).astype(BF16)
    send(S_KF, tf.at[1 - core], cf, kdev)

    for k in range(3):
        recv(S_ACT + k, act.at[rows(lax.rem(x + 3 - k, NX) * 64, 64), 128:640], xdev[2 - k])
    recv(S_KF, cf, kdev)
    uf[...] = (tf[core].astype(F32) + cf[...].astype(F32)).astype(BF16)
    for k in range(3):
        send(S_YF + k, uf.at[lax.rem(y + k + 1, NY)], yf.at[k], ydev[k])
    for j in range(4):
        for kh in range(3):
            tile = shifted(act, j, kh)
            for kw in range(3):
                row = 256 * (3 * kh + kw)
                x9[row : row + 256, 128 * j : 128 * j + 128] = tile[:, 128 * kw : 128 * kw + 128]
    grads = dot_t(c3[:, 128:640], x9[...])
    rsg[0:32, 0:2304] = grads[0:32]
    rsg[0:32, 2304:3456] = grads[32:64, 0:1152]
    rsg[32:64, 0:1152] = grads[32:64, 1152:2304]
    rsg[32:64, 1152:3456] = grads[64:96]
    rsg[:, 3456:3584] = jnp.zeros((64, 128), F32)
    for k in range(32):
        piece = rsg[:, 108 * k : 108 * k + 128].astype(BF16)
        ts[k % 2, (k % 8) // 2, k // 8] = piece[0:32]
        ts[k % 2, (k % 8) // 2, k // 8 + 4] = piece[32:64]
    send(S_KS, ts.at[1 - core], cs, kdev)

    total = uf[y].astype(F32)
    for k in range(3):
        recv(S_YF + k, yf.at[k], ydev[2 - k])
        total = total + yf[k].astype(F32)
    vf[...] = total.astype(BF16)
    for k in range(7):
        send(S_ZF + k, vf.at[lax.rem(zl + k + 1, 4)], zf.at[k], zldev[k])

    recv(S_KS, cs, kdev)
    us[...] = (ts[core].astype(F32) + cs[...].astype(F32)).astype(BF16)
    for k in range(3):
        send(S_YS + k, us.at[lax.rem(y + k + 1, NY)], yg.at[k], ydev[k])

    out = dot(w2s[...], x9[...])
    ys[0:32] = out[0:32].astype(BF16)
    ys[32:64] = out[64:96].astype(BF16)
    send(S_Y, ys.at[0:32], yr.at[0], up, jnp.logical_not(last))
    send(S_Y + 1, ys.at[32:64], yr.at[1], down, jnp.logical_not(first))

    total = us[y].astype(F32)
    for k in range(3):
        recv(S_YS + k, yg.at[k], ydev[2 - k])
        total = total + yg[k].astype(F32)
    vs[...] = total.astype(BF16)
    for k in range(7):
        send(S_ZS + k, vs.at[lax.rem(zl + k + 1, NZ)], zs.at[k], zldev[k])

    recv(S_Y, yr.at[0], down, jnp.logical_not(first))
    recv(S_Y + 1, yr.at[1], up, jnp.logical_not(last))
    before = jnp.where(first, 0.0, yr[0].astype(F32))
    after = jnp.where(last, 0.0, yr[1].astype(F32))
    so[...] = (out[32:64] + before + after).astype(BF16)

    total = vf[lax.rem(zl, 4)].astype(F32)
    for k in range(7):
        recv(S_ZF + k, zf.at[k], zldev[6 - k])
        total = total + zf[k].astype(F32)
    fgo[...] = jnp.where(zl < 4, total[:, 0:54], total[:, 64:118])
    total = vs[zl].astype(F32)
    for k in range(7):
        recv(S_ZS + k, zs.at[k], zldev[6 - k])
        total = total + zs[k].astype(F32)
    sgo[...] = total[:, 0:108]

    for copy, cond in pending:
        if cond is None:
            copy.wait_send()
        else:
            pl.when(cond)(copy.wait_send)


def shards(sample, first_weight, second_weight, cotangent):
    vmem = pl.BlockSpec(memory_space=pltpu.VMEM)
    hbm = pl.BlockSpec(memory_space=pltpu.HBM)
    b16 = [
        (16, 2, 16, 128), (32, 3456), (32, 6912), (32, 1, 8, 64), (32, 16, 128), (32, 512), (33, 128, 128),
        (2, 1152, 512), (96, 768), (864, 512), (864, 256),
    ]
    scratch = [pltpu.VMEM(shape, BF16) for shape in b16]
    scratch += [pltpu.VMEM((256, 512), F32)]
    scratch += [pltpu.VMEM((256, 512), BF16), pltpu.VMEM((3, 64, 512), BF16), pltpu.VMEM((64, 512), F32)]
    scratch += [pltpu.VMEM((64, 512), BF16), pltpu.VMEM((32, 512), BF16)]
    scratch += [pltpu.VMEM((8, 4, 2, 16, 128), BF16)] * 2
    scratch += [pltpu.VMEM((128, 1152), BF16), pltpu.VMEM((64, 1152), BF16)]
    scratch += [pltpu.VMEM((64, 512), F32)] * 3
    scratch += [pltpu.VMEM(shape, BF16) for shape in ((256, 768), (64, 512), (2304, 512), (96, 2304), (64, 512), (2, 32, 512))]
    scratch += [pltpu.VMEM((64, 3584), F32), pltpu.VMEM((32, 3584), F32)]
    for n in (4, 8):
        shapes = ((2, 4, n), (4, n), (4, n), (3, n), (n,), (7,))
        scratch += [pltpu.VMEM(shape + (32, 128), BF16) for shape in shapes]
    scratch += [pltpu.SemaphoreType.DMA((N_SEM,))] * 2 + [pltpu.SemaphoreType.DMA((4,))]
    so, fgo, sgo = pl.pallas_call(
        kernel,
        out_shape=(
            jax.ShapeDtypeStruct((32, 512), BF16),
            jax.ShapeDtypeStruct((32, 54), F32),
            jax.ShapeDtypeStruct((32, 108), F32),
        ),
        in_specs=[hbm] * 4,
        out_specs=(vmem, vmem, vmem),
        scratch_shapes=scratch,
        compiler_params=pltpu.CompilerParams(collective_id=0, has_side_effects=True, vmem_limit_bytes=48 * 1024 * 1024),
        name="slab_pair",
    )(sample, first_weight, second_weight, cotangent)
    return so.reshape(32, 1, 8, 64), fgo, sgo


def solution(mesh):
    return jax.shard_map(
        shards,
        mesh=mesh,
        in_specs=(
            P("chan", "depth", None, None),
            P("chan", None),
            P("chan", None),
            P("chan", "depth", None, None),
        ),
        out_specs=(P("chan", "depth", None, None), P("chan", "depth"), P("chan", "depth")),
        check_vma=False,
    )
```

time: 79 us -> 74.7 us (0.946)
  Pallas kernels: 73.2 us -> 68.1 us
    pallas_call x1, Pallas kernels: 73.2 us -> 68.1 us  [shards(): pl.pallas_call(kernel, out_shape=(jax.ShapeDtypeStruct((32, 512), BF16),...]
    unnamed x6 -> x10, local copies, waits for them, and re-layouts: 2.22 us -> 4.89 us
    reshape x1 -> x0, local copies, waits for them, and re-layouts: 1 us -> none  [shards(): cotangent.reshape(32, 512)]
    transpose x1 -> x0, local copies, waits for them, and re-layouts: 0.96 us -> none  [shards(): samp = sample.transpose(1, 2, 0, 3).reshape(32, 16, 128)]
where the time goes in v2:
time: 74.7 us; the launch traced here: 74.4 us
  Pallas kernels  68.1 us (91%)
  local copies, waits for them, and re-layouts  5.63 us (8%)
    pallas_call x1, Pallas kernels, shards(): pl.pallas_call(kernel, out_shape=(jax.ShapeDtypeStruct((32, 512), BF16),...  68.1 us
    unnamed x10, local copies, waits for them, and re-layouts  4.89 us

profile of v2, /device:TPU:1, one launch (start us, length us, event | category | flops | bytes accessed | tf_op | source)
XLA Modules:
  0.0 74.4 jit_solution(12952555423125104386)
XLA Ops:
  0.6 0.0 copy-start
  0.6 1.0 %copy-done = bf16[32,6912]{1,0:T(8,128)(2,1)S(1)} copy-done((bf16[32,6912]{1,0:T(8,128)(2,1)S(1)}, bf16[32,6912]{1,0:T(8,128)(2,1)}, u32[]{:S(2)}) %copy-start) | copy-done | bytes 442392
  1.6 0.0 copy-start.1
  1.6 0.9 %copy-done.1 = bf16[32,3456]{1,0:T(8,128)(2,1)S(1)} copy-done((bf16[32,3456]{1,0:T(8,128)(2,1)S(1)}, bf16[32,3456]{1,0:T(8,128)(2,1)}, u32[]{:S(2)}) %copy-start.1) | copy-done | bytes 221208
  2.6 0.0 copy-start.2
  2.6 0.9 %copy-done.2 = bf16[16,2,16,128]{3,2,1,0:T(8,128)(2,1)S(1)} copy-done((bf16[16,2,16,128]{3,2,1,0:T(8,128)(2,1)S(1)}, bf16[16,2,16,128]{3,2,1,0:T(8,128)(2,1)}, u32[]{:S(2)}) %copy-start.2) | copy-done | bytes 131096
  3.5 0.0 copy-start.3
  3.5 0.8 %copy-done.3 = bf16[32,1,8,64]{3,2,1,0:T(8,128)(2,1)S(1)} copy-done((bf16[32,1,8,64]{3,2,1,0:T(8,128)(2,1)S(1)}, bf16[32,1,8,64]{3,2,1,0:T(8,128)(2,1)}, u32[]{:S(2)}) %copy-start.3) | copy-done | bytes 32792
  4.3 68.1 %slab_pair.1 = (bf16[32,512]{1,0:T(8,128)(2,1)S(1)}, f32[32,54]{1,0:T(8,128)S(1)}, f32[32,108]{1,0:T(8,128)S(1)}) custom-call(bf16[16,2,16,128]{3,2,1,0:T(8,128)(2,1)S(1)} %copy-done.2, bf16[32,3456]{1,0:T(8,128)(2,1)S(1)} %copy-done.1, bf16[32,6912]{1,0:T(8,128)(2,1)S(1)} %copy-done, bf16[32,1,8,64]{3,2,1,0:T(8,128)(2,1)S(1)} %copy-done.3), custom_call_target="tpu_custom_call" | custom-call | tf_op jit(solution)/shard_map/slab_pair/pallas_call | solution.py:411
  72.4 0.7 reshape.9
  73.2 0.6 copy.10
  73.8 0.6 copy.11
Async XLA Ops:
  0.6 1.0 %copy-start = (bf16[32,6912]{1,0:T(8,128)(2,1)S(1)}, bf16[32,6912]{1,0:T(8,128)(2,1)}, u32[]{:S(2)}) copy-start(bf16[32,6912]{1,0:T(8,128)(2,1)} %w2_hbm.1) | copy-start | bytes 1327108
  1.6 0.9 %copy-start.1 = (bf16[32,3456]{1,0:T(8,128)(2,1)S(1)}, bf16[32,3456]{1,0:T(8,128)(2,1)}, u32[]{:S(2)}) copy-start(bf16[32,3456]{1,0:T(8,128)(2,1)} %w1_hbm.1) | copy-start | bytes 663556
  2.6 0.9 %copy-start.2 = (bf16[16,2,16,128]{3,2,1,0:T(8,128)(2,1)S(1)}, bf16[16,2,16,128]{3,2,1,0:T(8,128)(2,1)}, u32[]{:S(2)}) copy-start(bf16[16,2,16,128]{3,2,1,0:T(8,128)(2,1)} %samp_hbm.1) | copy-start | bytes 393220
  3.5 0.8 %copy-start.3 = (bf16[32,1,8,64]{3,2,1,0:T(8,128)(2,1)S(1)}, bf16[32,1,8,64]{3,2,1,0:T(8,128)(2,1)}, u32[]{:S(2)}) copy-start(bf16[32,1,8,64]{3,2,1,0:T(8,128)(2,1)} %cot_hbm.1) | copy-start | bytes 98308

commit v3 on v2

--- a/solution.py
+++ b/solution.py
@@ -30,10 +30,11 @@
 S_ZF = 39
 S_ZS = 46
 S_WZ = 53
-S_WL = 54
-S_WY = 61
-S_WK = 64
-N_SEM = 65
+S_WY = 54
+S_WK = 57
+N_SEM = 58
+
+VMEM_BYTES = 64 * 1024 * 1024 - 16 * 1024
 
 CHUNKS = ((16, 32), (7, 16), (0, 7))
 
@@ -153,14 +154,15 @@
         pair = jnp.concatenate([lines[64 * j : 64 * j + 32], lines[64 * j + 32 : 64 * j + 64]], axis=1)
         cot[:, 128 * j : 128 * j + 128] = pair.astype(BF16)
     loads[2].wait()
-    wo[...] = jnp.zeros(wo.shape, BF16)
-    for k in range(27):
-        wo[k // 4, k % 4] = w1[:, 128 * k : 128 * k + 128].reshape(2, 16, 128)
+    wo[3, 1] = jnp.zeros((7, 16, 128), BF16)
+    for k in range(54):
+        at = 16 * (k % 2)
+        wo[k // 14, k // 7 % 2, k % 7] = w1[at : at + 16, 128 * (k // 2) : 128 * (k // 2) + 128]
     pl.semaphore_wait(barrier, len(partners))
 
-    send(S_WZ, wo.at[zl, y, core], wp.at[zl, y, core], zdev)
-    for i, lines in enumerate(CHUNKS):
-        send(S_Z + i, own.at[lines[0] : lines[1]], sample_block(c, lines), zdev)
+    send(S_WZ, wo.at[y, core], wp.at[y, core], zdev)
+    over = [desc(S_Z + i, own.at[a:b], sample_block(c, (a, b)), zdev) for i, (a, b) in enumerate(CHUNKS)]
+    over[0].start()
     send(S_COT, cot, c3.at[64:96, 128:640], up, jnp.logical_not(last))
     send(S_COT + 1, cot, c3.at[0:32, 128:640], down, jnp.logical_not(first))
     for i, lines in enumerate(((16, 32), (0, 16))):
@@ -218,16 +220,21 @@
     for k in range(3):
         send(S_AGX + k, agb.at[rows(lax.rem(x + k + 1, NX) * 64, 64)], agr.at[k], xdev[k])
 
-    recv(S_WZ, wp.at[zl, y, core], zdev)
-    for k in range(7):
-        send(S_WL + k, wp.at[zl, y, core], wp.at[zl, y, core], zldev[k])
-
+    over[0].wait_send()
+    over[1].start()
+    recv(S_WZ, wp.at[y, core], zdev)
+    for k in range(3):
+        send(S_WY + k, wp.at[y, core], wp.at[y, core], ydev[k])
+
+    over[1].wait_send()
+    over[2].start()
     total = ag32[rows(x * 64, 64)]
     for k in range(3):
         recv(S_AGX + k, agr.at[k], xdev[2 - k])
         total = total + agr[k].astype(F32)
     az32[...] = total
     azb[...] = total.astype(BF16)
+    over[2].wait_send()
     send(S_AGZ, azb.at[pl.ds(theirs, 32)], azr, zdev)
 
     def across(i):
@@ -241,18 +248,14 @@
             recv(S_FX + 3 * i + k, sample_block(chan_at(3 - k, True), CHUNKS[i]), xdev[2 - k])
 
     across(0)
-    for k in range(7):
-        recv(S_WL + k, wp.at[lax.rem(zl + 7 - k, NZ), y, core], zldev[6 - k])
-    for k in range(3):
-        send(S_WY + k, wp.at[:, y, core], wp.at[:, y, core], ydev[k])
+    for k in range(3):
+        recv(S_WY + k, wp.at[lax.rem(y + 3 - k, NY), core], ydev[2 - k])
+    send(S_WK, wp.at[:, core], wp.at[:, core], kdev)
     across(1)
     across(2)
     for i, lines in enumerate(((16, 32), (0, 16))):
         for k in range(3):
             recv(S_OX + 3 * i + k, sample_block(chan_at(3 - k), lines), xdev[2 - k])
-    for k in range(3):
-        recv(S_WY + k, wp.at[:, lax.rem(y + 3 - k, NY), core], ydev[2 - k])
-    send(S_WK, wp.at[:, :, core], wp.at[:, :, core], kdev)
     stride = stride_matrix()
 
     def strided(plane, j):
@@ -267,14 +270,15 @@
     arrived(0)
     for j in range(4):
         strided(1, j)
-    recv(S_WK, wp.at[:, :, 1 - core], kdev)
-    for k in range(27):
-        tile = wp[k // 4, k % 4].reshape(32, 128)
-        at = 128 * (k % 9)
-        if k // 9 == 1:
-            w1m[pl.ds(theirs, 32), at : at + 128] = tile
+    recv(S_WK, wp.at[:, 1 - core], kdev)
+    for k in range(54):
+        tile = wp[k // 14, k // 7 % 2, k % 7]
+        at = 128 * (k // 2 % 9)
+        row = theirs + 16 * (k % 2)
+        if k // 18 == 1:
+            w1m[pl.ds(row, 16), at : at + 128] = tile
         else:
-            w1p[pl.ds(theirs + (64 if k < 9 else 0), 32), at : at + 128] = tile
+            w1p[pl.ds(row + (64 if k < 18 else 0), 16), at : at + 128] = tile
     both = dot(w1p[...], s[1])
     b1s[...] = both[64:128]
     send(S_B1, b1s, b1r, up, jnp.logical_not(last))
@@ -399,7 +403,7 @@
     scratch += [pltpu.VMEM((256, 512), F32)]
     scratch += [pltpu.VMEM((256, 512), BF16), pltpu.VMEM((3, 64, 512), BF16), pltpu.VMEM((64, 512), F32)]
     scratch += [pltpu.VMEM((64, 512), BF16), pltpu.VMEM((32, 512), BF16)]
-    scratch += [pltpu.VMEM((8, 4, 2, 16, 128), BF16)] * 2
+    scratch += [pltpu.VMEM((4, 2, 7, 16, 128), BF16)] * 2
     scratch += [pltpu.VMEM((128, 1152), BF16), pltpu.VMEM((64, 1152), BF16)]
     scratch += [pltpu.VMEM((64, 512), F32)] * 3
     scratch += [pltpu.VMEM(shape, BF16) for shape in ((256, 768), (64, 512), (2304, 512), (96, 2304), (64, 512), (2, 32, 512))]
@@ -418,7 +422,7 @@
         in_specs=[hbm] * 4,
         out_specs=(vmem, vmem, vmem),
         scratch_shapes=scratch,
-        compiler_params=pltpu.CompilerParams(collective_id=0, has_side_effects=True, vmem_limit_bytes=48 * 1024 * 1024),
+        compiler_params=pltpu.CompilerParams(collective_id=0, has_side_effects=True, vmem_limit_bytes=VMEM_BYTES),
         name="slab_pair",
     )(sample, first_weight, second_weight, cotangent)
     return so.reshape(32, 1, 8, 64), fgo, sgo

time: 74.7 us -> 67.4 us (0.902)
  Pallas kernels: 68.1 us -> 63.5 us
  local copies, waits for them, and re-layouts: 5.63 us -> 2.83 us
    pallas_call x1, Pallas kernels: 68.1 us -> 63.5 us  [shards(): pl.pallas_call(kernel, out_shape=(jax.ShapeDtypeStruct((32, 512), BF16),...]
    unnamed x10 -> x6, local copies, waits for them, and re-layouts: 4.89 us -> 1.33 us
    reshape x1, local copies, waits for them, and re-layouts: 0.74 us -> 1.5 us  [shards(): return (so.reshape(32, 1, 8, 64), fgo, sgo)]
where the time goes in v3:
time: 67.4 us; the launch traced here: 67 us
  Pallas kernels  63.5 us (94%)
  local copies, waits for them, and re-layouts  2.83 us (4%)
    pallas_call x1, Pallas kernels, shards(): pl.pallas_call(kernel, out_shape=(jax.ShapeDtypeStruct((32, 512), BF16),...  63.5 us
    reshape x1, local copies, waits for them, and re-layouts, shards(): return (so.reshape(32, 1, 8, 64), fgo, sgo)  1.5 us

profile of v3, /device:TPU:1, one launch (start us, length us, event | category | flops | bytes accessed | tf_op | source)
XLA Modules:
  0.0 67.0 jit_solution(16003058114169351403)
XLA Ops:
  0.6 63.5 %slab_pair.1 = (bf16[32,512]{1,0:T(8,128)(2,1)}, f32[32,54]{1,0:T(8,128)}, f32[32,108]{1,0:T(8,128)}) custom-call(bf16[16,2,16,128]{3,2,1,0:T(8,128)(2,1)} %samp_hbm.1, bf16[32,3456]{1,0:T(8,128)(2,1)} %w1_hbm.1, bf16[32,6912]{1,0:T(8,128)(2,1)} %w2_hbm.1, bf16[32,1,8,64]{3,2,1,0:T(8,128)(2,1)} %cot_hbm.1), custom_call_target="tpu_custom_call" | custom-call | tf_op jit(solution)/shard_map/slab_pair/pallas_call | solution.py:415
  64.1 0.0 copy-start.1
  64.1 1.5 %reshape.9 = bf16[32,1,8,64]{3,2,0,1:T(8,128)(2,1)} reshape(bf16[32,512]{1,0:T(8,128)(2,1)} %get-tuple-element.6) | data formatting | bytes 65536 | tf_op jit(solution)/shard_map/reshape | solution.py:428
  65.6 0.0 copy-done.1
  65.6 0.0 copy-start
  65.6 0.6 copy.10
  66.2 0.1 copy-done
  66.4 0.6 copy.11
Async XLA Ops:
  64.1 1.5 %copy-start.1 = (f32[32,54]{1,0:T(8,128)S(1)}, f32[32,54]{1,0:T(8,128)}, u32[]{:S(2)}) copy-start(f32[32,54]{1,0:T(8,128)} %get-tuple-element.16) | copy-start | bytes 20740
  65.6 0.7 %copy-start = (f32[32,108]{1,0:T(8,128)S(1)}, f32[32,108]{1,0:T(8,128)}, u32[]{:S(2)}) copy-start(f32[32,108]{1,0:T(8,128)} %get-tuple-element.17) | copy-start | bytes 41476

commit v4 on v3

--- a/solution.py
+++ b/solution.py
@@ -252,7 +252,6 @@
         recv(S_WY + k, wp.at[lax.rem(y + 3 - k, NY), core], ydev[2 - k])
     send(S_WK, wp.at[:, core], wp.at[:, core], kdev)
     across(1)
-    across(2)
     for i, lines in enumerate(((16, 32), (0, 16))):
         for k in range(3):
             recv(S_OX + 3 * i + k, sample_block(chan_at(3 - k), lines), xdev[2 - k])
@@ -282,6 +281,7 @@
     both = dot(w1p[...], s[1])
     b1s[...] = both[64:128]
     send(S_B1, b1s, b1r, up, jnp.logical_not(last))
+    across(2)
     arrived(1)
     halves = [None, None]
     for half in (1, 0):
@@ -296,7 +296,7 @@
     sl = jnp.where(pre > 0, 1.0, LEAK)
     group = act.at[rows(x * 64, 64), 128:640]
     group[...] = (pre * sl).astype(BF16)
-    for k in range(3):
+    for k in (1, 0, 2):
         send(S_ACT + k, group, group, xdev[k])
     slope[...] = sl
 
@@ -341,6 +341,15 @@
         ts[k % 2, (k % 8) // 2, k // 8 + 4] = piece[32:64]
     send(S_KS, ts.at[1 - core], cs, kdev)
 
+    recv(S_KS, cs, kdev)
+    us[...] = (ts[core].astype(F32) + cs[...].astype(F32)).astype(BF16)
+    for k in (1, 0, 2):
+        send(S_YS + k, us.at[lax.rem(y + k + 1, NY)], yg.at[k], ydev[k])
+
+    out = dot(w2s[...], x9[...])
+    ys[0:32] = out[0:32].astype(BF16)
+    ys[32:64] = out[64:96].astype(BF16)
+
     total = uf[y].astype(F32)
     for k in range(3):
         recv(S_YF + k, yf.at[k], ydev[2 - k])
@@ -349,17 +358,6 @@
     for k in range(7):
         send(S_ZF + k, vf.at[lax.rem(zl + k + 1, 4)], zf.at[k], zldev[k])
 
-    recv(S_KS, cs, kdev)
-    us[...] = (ts[core].astype(F32) + cs[...].astype(F32)).astype(BF16)
-    for k in range(3):
-        send(S_YS + k, us.at[lax.rem(y + k + 1, NY)], yg.at[k], ydev[k])
-
-    out = dot(w2s[...], x9[...])
-    ys[0:32] = out[0:32].astype(BF16)
-    ys[32:64] = out[64:96].astype(BF16)
-    send(S_Y, ys.at[0:32], yr.at[0], up, jnp.logical_not(last))
-    send(S_Y + 1, ys.at[32:64], yr.at[1], down, jnp.logical_not(first))
-
     total = us[y].astype(F32)
     for k in range(3):
         recv(S_YS + k, yg.at[k], ydev[2 - k])
@@ -368,6 +366,8 @@
     for k in range(7):
         send(S_ZS + k, vs.at[lax.rem(zl + k + 1, NZ)], zs.at[k], zldev[k])
 
+    send(S_Y, ys.at[0:32], yr.at[0], up, jnp.logical_not(last))
+    send(S_Y + 1, ys.at[32:64], yr.at[1], down, jnp.logical_not(first))
     recv(S_Y, yr.at[0], down, jnp.logical_not(first))
     recv(S_Y + 1, yr.at[1], up, jnp.logical_not(last))
     before = jnp.where(first, 0.0, yr[0].astype(F32))

time: 67.4 us -> 67.3 us (level)
  no operation moved by 1% of the time
where the time goes in v4:
time: 67.3 us; the launch traced here: 67 us
  Pallas kernels  63.5 us (94%)
  local copies, waits for them, and re-layouts  2.83 us (4%)
    pallas_call x1, Pallas kernels, shards(): pl.pallas_call(kernel, out_shape=(jax.ShapeDtypeStruct((32, 512), BF16),...  63.5 us
    reshape x1, local copies, waits for them, and re-layouts, shards(): return (so.reshape(32, 1, 8, 64), fgo, sgo)  1.5 us

profile of v4, /device:TPU:1, one launch (start us, length us, event | category | flops | bytes accessed | tf_op | source)
XLA Modules:
  0.0 67.0 jit_solution(18438691799407134667)
XLA Ops:
  0.6 63.5 %slab_pair.1 = (bf16[32,512]{1,0:T(8,128)(2,1)}, f32[32,54]{1,0:T(8,128)}, f32[32,108]{1,0:T(8,128)}) custom-call(bf16[16,2,16,128]{3,2,1,0:T(8,128)(2,1)} %samp_hbm.1, bf16[32,3456]{1,0:T(8,128)(2,1)} %w1_hbm.1, bf16[32,6912]{1,0:T(8,128)(2,1)} %w2_hbm.1, bf16[32,1,8,64]{3,2,1,0:T(8,128)(2,1)} %cot_hbm.1), custom_call_target="tpu_custom_call" | custom-call | tf_op jit(solution)/shard_map/slab_pair/pallas_call | solution.py:415
  64.2 0.0 copy-start.1
  64.2 1.5 %reshape.9 = bf16[32,1,8,64]{3,2,0,1:T(8,128)(2,1)} reshape(bf16[32,512]{1,0:T(8,128)(2,1)} %get-tuple-element.6) | data formatting | bytes 65536 | tf_op jit(solution)/shard_map/reshape | solution.py:428
  65.7 0.0 copy-done.1
  65.7 0.0 copy-start
  65.7 0.6 copy.10
  66.3 0.1 copy-done
  66.4 0.6 copy.11
Async XLA Ops:
  64.2 1.5 %copy-start.1 = (f32[32,54]{1,0:T(8,128)S(1)}, f32[32,54]{1,0:T(8,128)}, u32[]{:S(2)}) copy-start(f32[32,54]{1,0:T(8,128)} %get-tuple-element.16) | copy-start | bytes 20740
  65.7 0.7 %copy-start = (f32[32,108]{1,0:T(8,128)S(1)}, f32[32,108]{1,0:T(8,128)}, u32[]{:S(2)}) copy-start(f32[32,108]{1,0:T(8,128)} %get-tuple-element.17) | copy-start | bytes 41476

commit v5 on v4

--- a/solution.py
+++ b/solution.py
@@ -166,7 +166,7 @@
     send(S_COT, cot, c3.at[64:96, 128:640], up, jnp.logical_not(last))
     send(S_COT + 1, cot, c3.at[0:32, 128:640], down, jnp.logical_not(first))
     for i, lines in enumerate(((16, 32), (0, 16))):
-        for k in range(3):
+        for k in (1, 0, 2):
             send(S_OX + 3 * i + k, own.at[lines[0] : lines[1]], sample_block(c, lines), xdev[k])
 
     c3[:, 0:128] = jnp.zeros((96, 128), BF16)
@@ -217,7 +217,7 @@
     part = lax.dot_general(wv[...], ci[...], (((0,), (0,)), ((), ())), preferred_element_type=F32)
     ag32[...] = part
     agb[...] = part.astype(BF16)
-    for k in range(3):
+    for k in (1, 0, 2):
         send(S_AGX + k, agb.at[rows(lax.rem(x + k + 1, NX) * 64, 64)], agr.at[k], xdev[k])
 
     over[0].wait_send()
@@ -240,7 +240,7 @@
     def across(i):
         block = sample_block(chan_at(0, True), CHUNKS[i])
         recv(S_Z + i, block, zdev)
-        for k in range(3):
+        for k in (1, 0, 2):
             send(S_FX + 3 * i + k, block, block, xdev[k])
 
     def arrived(i):
@@ -321,7 +321,7 @@
         recv(S_ACT + k, act.at[rows(lax.rem(x + 3 - k, NX) * 64, 64), 128:640], xdev[2 - k])
     recv(S_KF, cf, kdev)
     uf[...] = (tf[core].astype(F32) + cf[...].astype(F32)).astype(BF16)
-    for k in range(3):
+    for k in (1, 0, 2):
         send(S_YF + k, uf.at[lax.rem(y + k + 1, NY)], yf.at[k], ydev[k])
     for j in range(4):
         for kh in range(3):
@@ -372,7 +372,9 @@
     recv(S_Y + 1, yr.at[1], up, jnp.logical_not(last))
     before = jnp.where(first, 0.0, yr[0].astype(F32))
     after = jnp.where(last, 0.0, yr[1].astype(F32))
-    so[...] = (out[32:64] + before + after).astype(BF16)
+    rounded = (out[32:64] + before + after).astype(BF16)
+    lines = jnp.concatenate([rounded[:, 64 * h : 64 * h + 64] for h in range(8)], axis=0)
+    so[:, 0] = dot(swap_matrix(256, 8), lines).reshape(32, 8, 64).astype(BF16)
 
     total = vf[lax.rem(zl, 4)].astype(F32)
     for k in range(7):
@@ -415,7 +417,7 @@
     so, fgo, sgo = pl.pallas_call(
         kernel,
         out_shape=(
-            jax.ShapeDtypeStruct((32, 512), BF16),
+            jax.ShapeDtypeStruct((32, 1, 8, 64), BF16),
             jax.ShapeDtypeStruct((32, 54), F32),
             jax.ShapeDtypeStruct((32, 108), F32),
         ),
@@ -425,7 +427,7 @@
         compiler_params=pltpu.CompilerParams(collective_id=0, has_side_effects=True, vmem_limit_bytes=VMEM_BYTES),
         name="slab_pair",
     )(sample, first_weight, second_weight, cotangent)
-    return so.reshape(32, 1, 8, 64), fgo, sgo
+    return so, fgo, sgo
 
 
 def solution(mesh):

time: 67.3 us -> 66.8 us (level)
    reshape x1 -> x0, local copies, waits for them, and re-layouts: 1.5 us -> none  [shards(): return (so.reshape(32, 1, 8, 64), fgo, sgo)]
    unnamed x6 -> x7, local copies, waits for them, and re-layouts: 1.33 us -> 2.81 us
where the time goes in v5:
time: 66.8 us; the launch traced here: 66.5 us
  Pallas kernels  63.1 us (94%)
  local copies, waits for them, and re-layouts  2.81 us (4%)
    pallas_call x1, Pallas kernels, shards(): pl.pallas_call(kernel, out_shape=(jax.ShapeDtypeStruct((32, 1, 8, 64), BF...  63.1 us
    unnamed x7, local copies, waits for them, and re-layouts  2.81 us

profile of v5, /device:TPU:1, one launch (start us, length us, event | category | flops | bytes accessed | tf_op | source)
XLA Modules:
  0.0 66.5 jit_solution(14310059983909091029)
XLA Ops:
  0.6 63.1 %slab_pair.1 = (bf16[32,1,8,64]{3,2,1,0:T(8,128)(2,1)}, f32[32,54]{1,0:T(8,128)}, f32[32,108]{1,0:T(8,128)}) custom-call(bf16[16,2,16,128]{3,2,1,0:T(8,128)(2,1)} %samp_hbm.1, bf16[32,3456]{1,0:T(8,128)(2,1)} %w1_hbm.1, bf16[32,6912]{1,0:T(8,128)(2,1)} %w2_hbm.1, bf16[32,1,8,64]{3,2,1,0:T(8,128)(2,1)} %cot_hbm.1), custom_call_target="tpu_custom_call" | custom-call | tf_op jit(solution)/shard_map/slab_pair/pallas_call | solution.py:417
  63.7 0.0 copy-start.1
  63.7 1.5 %copy.10 = bf16[32,1,8,64]{3,2,1,0:T(8,128)(2,1)} copy(bf16[32,1,8,64]{3,2,1,0:T(8,128)(2,1)} %get-tuple-element.6) | data formatting | bytes 65536
  65.2 0.0 copy-done.1
  65.2 0.0 copy-start
  65.2 0.6 copy.11
  65.8 0.1 copy-done
  65.9 0.6 copy.12
Async XLA Ops:
  63.7 1.5 %copy-start.1 = (f32[32,54]{1,0:T(8,128)S(1)}, f32[32,54]{1,0:T(8,128)}, u32[]{:S(2)}) copy-start(f32[32,54]{1,0:T(8,128)} %get-tuple-element.7) | copy-start | bytes 20740
  65.2 0.7 %copy-start = (f32[32,108]{1,0:T(8,128)S(1)}, f32[32,108]{1,0:T(8,128)}, u32[]{:S(2)}) copy-start(f32[32,108]{1,0:T(8,128)} %get-tuple-element.8) | copy-start | bytes 41476

commit v6 on v5

--- a/solution.py
+++ b/solution.py
@@ -160,15 +160,17 @@
         wo[k // 14, k // 7 % 2, k % 7] = w1[at : at + 16, 128 * (k // 2) : 128 * (k // 2) + 128]
     pl.semaphore_wait(barrier, len(partners))
 
-    send(S_WZ, wo.at[y, core], wp.at[y, core], zdev)
+    filt = desc(S_WZ, wo.at[y, core], wp.at[y, core], zdev)
+    filt.start()
     over = [desc(S_Z + i, own.at[a:b], sample_block(c, (a, b)), zdev) for i, (a, b) in enumerate(CHUNKS)]
-    over[0].start()
     send(S_COT, cot, c3.at[64:96, 128:640], up, jnp.logical_not(last))
     send(S_COT + 1, cot, c3.at[0:32, 128:640], down, jnp.logical_not(first))
     for i, lines in enumerate(((16, 32), (0, 16))):
         for k in (1, 0, 2):
             send(S_OX + 3 * i + k, own.at[lines[0] : lines[1]], sample_block(c, lines), xdev[k])
 
+    filt.wait_send()
+    over[0].start()
     c3[:, 0:128] = jnp.zeros((96, 128), BF16)
     c3[:, 640:768] = jnp.zeros((96, 128), BF16)
     act[:, 0:128] = jnp.zeros((256, 128), BF16)

time: 66.8 us -> 66.9 us (level)
  no operation moved by 1% of the time
where the time goes in v6:
time: 66.9 us; the launch traced here: 66.7 us
  Pallas kernels  63.2 us (94%)
  local copies, waits for them, and re-layouts  2.81 us (4%)
    pallas_call x1, Pallas kernels, shards(): pl.pallas_call(kernel, out_shape=(jax.ShapeDtypeStruct((32, 1, 8, 64), BF...  63.2 us
    unnamed x7, local copies, waits for them, and re-layouts  2.81 us

profile of v6, /device:TPU:1, one launch (start us, length us, event | category | flops | bytes accessed | tf_op | source)
XLA Modules:
  0.0 66.7 jit_solution(15130206278172600714)
XLA Ops:
  0.6 63.2 %slab_pair.1 = (bf16[32,1,8,64]{3,2,1,0:T(8,128)(2,1)}, f32[32,54]{1,0:T(8,128)}, f32[32,108]{1,0:T(8,128)}) custom-call(bf16[16,2,16,128]{3,2,1,0:T(8,128)(2,1)} %samp_hbm.1, bf16[32,3456]{1,0:T(8,128)(2,1)} %w1_hbm.1, bf16[32,6912]{1,0:T(8,128)(2,1)} %w2_hbm.1, bf16[32,1,8,64]{3,2,1,0:T(8,128)(2,1)} %cot_hbm.1), custom_call_target="tpu_custom_call" | custom-call | tf_op jit(solution)/shard_map/slab_pair/pallas_call | solution.py:419
  63.8 0.0 copy-start.1
  63.9 1.5 %copy.10 = bf16[32,1,8,64]{3,2,1,0:T(8,128)(2,1)} copy(bf16[32,1,8,64]{3,2,1,0:T(8,128)(2,1)} %get-tuple-element.6) | data formatting | bytes 65536
  65.3 0.0 copy-done.1
  65.3 0.0 copy-start
  65.3 0.6 copy.11
  65.9 0.1 copy-done
  66.1 0.6 copy.12
Async XLA Ops:
  63.8 1.5 %copy-start.1 = (f32[32,54]{1,0:T(8,128)S(1)}, f32[32,54]{1,0:T(8,128)}, u32[]{:S(2)}) copy-start(f32[32,54]{1,0:T(8,128)} %get-tuple-element.7) | copy-start | bytes 20740
  65.3 0.7 %copy-start = (f32[32,108]{1,0:T(8,128)S(1)}, f32[32,108]{1,0:T(8,128)}, u32[]{:S(2)}) copy-start(f32[32,108]{1,0:T(8,128)} %get-tuple-element.8) | copy-start | bytes 41476
